TPU v7x, 32 devices: a whole 2x2x4 slice. The times are simulated.
32 devices in a mesh: ctx: 8 (over z, x), dp: 4 (over y, core).
Axes of the slice: x: 2, y: 2, z: 4, core: 2. Of those that a mesh axis runs over, the one named last changes fastest.
Arguments:
- recurrent_probe_vectors: bfloat16 [4096, 4096], P(('dp', 'ctx')), parts along dimension 0, may hold values from -3 to 3
- recurrent_matcher_vectors: bfloat16 [4096, 4096], P(('dp', 'ctx')), parts along dimension 0, may hold values from -3 to 3
- recurrent_content_vectors: bfloat16 [4096, 4096], P(('dp', 'ctx')), parts along dimension 0, may hold values from -6 to 6
- recurrent_result_sensitivity: bfloat16 [4096, 4096], P(('dp', 'ctx')), parts along dimension 0, may hold values from -6 to 6
- attender_fade_power: int32 [128], P('dp'), parts along dimension 0, may hold values from 5 to 16
- surplus_fade_amounts: float32 [4096, 32], P(('dp', 'ctx')), parts along dimension 0, may hold values from -0.7 to 0
- normalized_probe_vectors: bfloat16 [4096, 4096], P(('dp', 'ctx')), parts along dimension 0, may hold values from -120 to 120
- normalized_matcher_vectors: bfloat16 [4096, 512], P(('dp', 'ctx')), parts along dimension 0, may hold values from -5 to 5
- normalized_content_vectors: bfloat16 [4096, 512], P(('dp', 'ctx')), parts along dimension 0, may hold values from -6 to 6
- normalized_result_sensitivity: bfloat16 [4096, 4096], P(('dp', 'ctx')), parts along dimension 0, may hold values from -6 to 6
Outputs:
- linear_query_grad: bfloat16 [4096, 4096], P(('dp', 'ctx')), parts along dimension 0
- linear_key_grad: bfloat16 [4096, 4096], P(('dp', 'ctx')), parts along dimension 0
- linear_value_grad: bfloat16 [4096, 4096], P(('dp', 'ctx')), parts along dimension 0
- softmax_query_grad: bfloat16 [4096, 4096], P(('dp', 'ctx')), parts along dimension 0
- softmax_key_grad: bfloat16 [4096, 512], P(('dp', 'ctx')), parts along dimension 0
- softmax_value_grad: bfloat16 [4096, 512], P(('dp', 'ctx')), parts along dimension 0
There are 4 independent parts, one for each index of `dp`. A program takes and returns all parts, laid end to end along the dimension named above; each array names one. Nothing has to cross between parts.
All inputs are finite; a program needn't handle non-finite values.
Results may differ from a plain program's by a relative error of at most 0.012.
Values may be sent and summed in bfloat16 or wider, within the bound.
A program may use at most 128 MiB of HBM per device.

v0:
```python
import jax
import jax.numpy as jnp
from jax import lax
from jax.sharding import PartitionSpec as P

G = 4


def passed_along(shard, axis, by):
    devices = lax.axis_size(axis)
    pairs = [(i, i + by) for i in range(devices) if 0 <= i + by < devices]
    return lax.ppermute(shard, axis, pairs)


def linear_local(query, keys, values, cotangent, fade_natural_rate):
    tokens = query.shape[0]
    number_of_attenders = fade_natural_rate.shape[1]
    width = query.shape[1] // number_of_attenders
    scale = 1.0 / width
    query_three = query.reshape(tokens, number_of_attenders, width)
    keys_three = keys.reshape(tokens, number_of_attenders, width)
    values_three = values.reshape(tokens, number_of_attenders, width)
    cotan_three = cotangent.reshape(tokens, number_of_attenders, width)
    cumul = jnp.cumsum(fade_natural_rate, axis=0)
    total = cumul[-1]
    heads_cumul = cumul.T
    spread = heads_cumul[:, :, None] - heads_cumul[:, None, :]
    causal = lax.broadcasted_iota(jnp.int32, (tokens, tokens), 0) >= lax.broadcasted_iota(
        jnp.int32, (tokens, tokens), 1
    )
    decay = jnp.where(causal[None], jnp.exp(jnp.minimum(spread, 0.0)), 0.0)
    outer_grad = jnp.einsum(
        "thd,shd->hts", cotan_three, values_three, preferred_element_type=jnp.float32
    )
    outer_score = jnp.einsum(
        "thd,shd->hts", query_three, keys_three, preferred_element_type=jnp.float32
    )
    mix_grad = (decay * outer_grad * scale).astype(jnp.bfloat16)
    mix_score = (decay * outer_score * scale).astype(jnp.bfloat16)
    inner_query = jnp.einsum(
        "hts,shd->thd", mix_grad, keys_three, preferred_element_type=jnp.float32
    )
    inner_key = jnp.einsum(
        "hts,thd->shd", mix_grad, query_three, preferred_element_type=jnp.float32
    )
    inner_value = jnp.einsum(
        "hts,thd->shd", mix_score, cotan_three, preferred_element_type=jnp.float32
    )
    to_end = jnp.exp(total[None, :] - cumul)
    from_start = jnp.exp(cumul)
    weighted_key = (keys_three * to_end[:, :, None]).astype(jnp.bfloat16)
    weighted_query = (query_three * from_start[:, :, None]).astype(jnp.bfloat16)
    key_state = jnp.einsum(
        "shd,she->hde", weighted_key, values_three, preferred_element_type=jnp.float32
    )
    grad_state = jnp.einsum(
        "thd,the->hde", weighted_query, cotan_three, preferred_element_type=jnp.float32
    )
    return (inner_query, inner_key, inner_value, key_state, grad_state, total, to_end, from_start)


def linear_finish(
    inner_query,
    inner_key,
    inner_value,
    key_in,
    grad_in,
    to_end,
    from_start,
    keys,
    values,
    cotangent,
):
    tokens, number_of_attenders, width = inner_query.shape
    scale = 1.0 / width
    keys_three = keys.reshape(tokens, number_of_attenders, width)
    values_three = values.reshape(tokens, number_of_attenders, width)
    cotan_three = cotangent.reshape(tokens, number_of_attenders, width)
    key_half = key_in.astype(jnp.bfloat16)
    grad_half = grad_in.astype(jnp.bfloat16)
    query_grad = inner_query + scale * from_start[:, :, None] * jnp.einsum(
        "hde,the->thd", key_half, cotan_three, preferred_element_type=jnp.float32
    )
    key_grad = inner_key + scale * to_end[:, :, None] * jnp.einsum(
        "hde,she->shd", grad_half, values_three, preferred_element_type=jnp.float32
    )
    value_grad = inner_value + scale * to_end[:, :, None] * jnp.einsum(
        "hde,shd->she", grad_half, keys_three, preferred_element_type=jnp.float32
    )
    flat = (tokens, number_of_attenders * width)
    return (
        query_grad.reshape(flat).astype(jnp.bfloat16),
        key_grad.reshape(flat).astype(jnp.bfloat16),
        value_grad.reshape(flat).astype(jnp.bfloat16),
    )


def combine_states(earlier, later):
    return (later[0] + jnp.exp(later[1])[:, None, None] * earlier[0], earlier[1] + later[1])


def softmax_block(query, cotangent, keys, values, visible, groups):
    rows = query.shape[0]
    width = keys.shape[1] // groups
    number_of_attenders = query.shape[1] // width
    share = number_of_attenders // groups
    scale = width ** (-0.5)
    query_groups = query.reshape(rows, groups, share, width).transpose(1, 0, 2, 3)
    cotan_groups = cotangent.reshape(rows, groups, share, width).transpose(1, 0, 2, 3)
    key_groups = keys.reshape(-1, groups, width).transpose(1, 0, 2)
    value_groups = values.reshape(-1, groups, width).transpose(1, 0, 2)

    def one_group(pieces):
        query_head, cotan_head, key_head, value_head = pieces
        score = (
            jnp.einsum("trd,sd->rts", query_head, key_head, preferred_element_type=jnp.float32)
            * scale
        )
        score = jnp.where(visible[None], score, -jnp.inf)
        peak = jnp.max(score, axis=2, keepdims=True)
        expo = jnp.exp(score - peak)
        prob = expo / jnp.sum(expo, axis=2, keepdims=True)
        prob_half = prob.astype(jnp.bfloat16)
        output = jnp.einsum(
            "rts,se->tre", prob_half, value_head, preferred_element_type=jnp.float32
        ).astype(jnp.bfloat16)
        output = lax.optimization_barrier(output)
        delta = jnp.sum(cotan_head.astype(jnp.float32) * output.astype(jnp.float32), axis=2)
        dprob = jnp.einsum(
            "tre,se->rts", cotan_head, value_head, preferred_element_type=jnp.float32
        )
        dscore = prob * (dprob - delta.T[:, :, None])
        dscore_half = dscore.astype(jnp.bfloat16)
        query_grad = (
            jnp.einsum("rts,sd->trd", dscore_half, key_head, preferred_element_type=jnp.float32)
            * scale
        )
        key_grad = (
            jnp.einsum("rts,trd->sd", dscore_half, query_head, preferred_element_type=jnp.float32)
            * scale
        )
        value_grad = jnp.einsum(
            "rts,tre->se", prob_half, cotan_head, preferred_element_type=jnp.float32
        )
        return (query_grad, key_grad, value_grad)

    query_grad, key_grad, value_grad = lax.map(
        one_group, (query_groups, cotan_groups, key_groups, value_groups)
    )
    query_grad = query_grad.transpose(1, 0, 2, 3).reshape(rows, number_of_attenders * width)
    key_grad = key_grad.transpose(1, 0, 2).reshape(-1, groups * width)
    value_grad = value_grad.transpose(1, 0, 2).reshape(-1, groups * width)
    return (query_grad, key_grad, value_grad)


def body(
    recurrent_probe_vectors,
    recurrent_matcher_vectors,
    recurrent_content_vectors,
    recurrent_result_sensitivity,
    attender_fade_power,
    surplus_fade_amounts,
    normalized_probe_vectors,
    normalized_matcher_vectors,
    normalized_content_vectors,
    normalized_result_sensitivity,
):
    rows = recurrent_probe_vectors.shape[0]
    number_of_attenders = surplus_fade_amounts.shape[1]
    width = recurrent_probe_vectors.shape[1] // number_of_attenders
    fade_natural_rate = (
        surplus_fade_amounts - jnp.power(2.0, -attender_fade_power.astype(jnp.float32))[None, :]
    )
    inner_query, inner_key, inner_value, key_state, grad_state, total, to_end, from_start = (
        linear_local(
            recurrent_probe_vectors,
            recurrent_matcher_vectors,
            recurrent_content_vectors,
            recurrent_result_sensitivity,
            fade_natural_rate,
        )
    )
    identity = (
        jnp.zeros((number_of_attenders, width, width), jnp.float32),
        jnp.zeros((number_of_attenders,), jnp.float32),
    )
    depth = lax.axis_size("ctx").bit_length() - 1
    offsets = [1] + [1 << level for level in range(depth)]
    source = (key_state, total)
    forward = identity
    for offset in offsets:
        moved = passed_along((source[0], source[1]), "ctx", offset)
        forward = combine_states(moved, forward)
        source = forward
    key_in = forward[0]
    source = (grad_state, total)
    backward = identity
    for offset in offsets:
        moved = passed_along((source[0], source[1]), "ctx", -offset)
        backward = combine_states(moved, backward)
        source = backward
    grad_in = backward[0]
    linear_query_grad, linear_key_grad, linear_value_grad = linear_finish(
        inner_query,
        inner_key,
        inner_value,
        key_in,
        grad_in,
        to_end,
        from_start,
        recurrent_matcher_vectors,
        recurrent_content_vectors,
        recurrent_result_sensitivity,
    )
    window = min(3, lax.axis_size("ctx") // 2)
    position = lax.axis_index("ctx")
    stacked = jnp.stack([normalized_matcher_vectors, normalized_content_vectors], axis=0)

    def pass_on(carry, unused):
        moved = passed_along(carry, "ctx", 1)
        return (moved, moved)

    _, earlier = lax.scan(pass_on, stacked, None, length=window - 1)
    blocks_kv = jnp.concatenate([stacked[None], earlier], axis=0)
    span = window * rows
    keys_all = blocks_kv[:, 0].reshape(span, -1)
    values_all = blocks_kv[:, 1].reshape(span, -1)
    slots = lax.broadcasted_iota(jnp.int32, (span,), 0) // rows
    within = lax.broadcasted_iota(jnp.int32, (span,), 0) % rows
    query_pos = lax.broadcasted_iota(jnp.int32, (rows,), 0)
    present = position - slots >= 0
    visible = present[None, :] & ((slots > 0)[None, :] | (within[None, :] <= query_pos[:, None]))
    query_grad, key_grad, value_grad = softmax_block(
        normalized_probe_vectors, normalized_result_sensitivity, keys_all, values_all, visible, G
    )
    grads = jnp.stack(
        [key_grad.reshape(window, rows, -1), value_grad.reshape(window, rows, -1)], axis=1
    )

    def collect(offset, accum):
        moved = passed_along(accum, "ctx", -1)
        return moved + lax.dynamic_index_in_dim(grads, window - 1 - offset, 0, keepdims=False)

    accum = lax.fori_loop(1, window, collect, grads[window - 1])
    softmax_query_grad = query_grad.astype(jnp.bfloat16)
    softmax_key_grad = accum[0].astype(jnp.bfloat16)
    softmax_value_grad = accum[1].astype(jnp.bfloat16)
    return (
        linear_query_grad,
        linear_key_grad,
        linear_value_grad,
        softmax_query_grad,
        softmax_key_grad,
        softmax_value_grad,
    )


def solution(mesh):
    placed = (
        P(("dp", "ctx"), None),
        P(("dp", "ctx"), None),
        P(("dp", "ctx"), None),
        P(("dp", "ctx"), None),
        P("dp"),
        P(("dp", "ctx"), None),
        P(("dp", "ctx"), None),
        P(("dp", "ctx"), None),
        P(("dp", "ctx"), None),
        P(("dp", "ctx"), None),
    )
    return jax.shard_map(
        body,
        mesh=mesh,
        in_specs=placed,
        out_specs=(
            P(("dp", "ctx"), None),
            P(("dp", "ctx"), None),
            P(("dp", "ctx"), None),
            P(("dp", "ctx"), None),
            P(("dp", "ctx"), None),
            P(("dp", "ctx"), None),
        ),
        check_vma=False,
    )
```

profile of v0, /device:TPU:16, one launch (start us, length us, event | category | flops | bytes accessed | tf_op | source)
XLA Modules:
  0.0 524.1 jit_solution(600256107016907235)
XLA Ops:
  10.2 3.3 collective-permute-start.9
  19.6 85.2 %collective-permute-done.9 = f32[32,128,128]{2,1,0:T(8,128)} collective-permute-done((f32[32,128,128]{2,1,0:T(8,128)}, f32[32,128,128]{2,1,0:T(8,128)}, u32[]{:S(2)}, u32[]{:S(2)}) %collective-permute-start.9) | collective-permute-done | bytes 2097184 | tf_op jit(solution)/shard_map/ppermute | solution.py:12
  106.7 3.8 collective-permute-start.10
  112.6 56.3 %while.42 = (s32[]{:T(128)}, bf16[2,128,512]{2,1,0:T(8,128)(2,1)S(1)}, bf16[2,2,128,512]{3,2,1,0:T(8,128)(2,1)S(1)}, s32[]{:T(128)}) while((s32[]{:T(128)}, bf16[2,128,512]{2,1,0:T(8,128)(2,1)S(1)}, bf16[2,2,128,512]{3,2,1,0:T(8,128)(2,1)S(1)}, s32[]{:T(128)}) %tuple.88), condition=%wide.region_2.3_spmd, body=%wide.region_1.2_spmd.sunk | while | flops 2 | bytes 2097257 | solution.py:223
  112.6 4.8 collective-permute-start
  117.5 40.3 %collective-permute-done = bf16[2,128,512]{2,1,0:T(8,128)(2,1)S(1)} collective-permute-done((bf16[2,128,512]{2,1,0:T(8,128)(2,1)S(1)}, bf16[2,128,512]{2,1,0:T(8,128)(2,1)S(1)}, u32[]{:S(2)}, u32[]{:S(2)}) %collective-permute-start) | collective-permute-done | bytes 262176 | tf_op jit(solution)/shard_map/while/body/eval_jaxpr/ppermute | solution.py:12
  157.9 4.4 collective-permute-start
  162.3 6.6 %collective-permute-done = bf16[2,128,512]{2,1,0:T(8,128)(2,1)S(1)} collective-permute-done((bf16[2,128,512]{2,1,0:T(8,128)(2,1)S(1)}, bf16[2,128,512]{2,1,0:T(8,128)(2,1)S(1)}, u32[]{:S(2)}, u32[]{:S(2)}) %collective-permute-start) | collective-permute-done | bytes 262176 | tf_op jit(solution)/shard_map/while/body/eval_jaxpr/ppermute | solution.py:12
  173.6 3.4 collective-permute-start.12
  180.5 4.3 collective-permute-start.4
  184.8 3.8 multiply_add_fusion.1
  190.9 54.4 %while.44 = (s32[]{:T(128)}, bf16[4,128,8,128]{1,3,2,0:T(8,128)(2,1)}, f32[4,384,128]{2,1,0:T(8,128)}, f32[4,384,128]{2,1,0:T(8,128)}, bf16[4,384,128]{2,1,0:T(8...) while((s32[]{:T(128)}, ...), condition=%wide.region_7.8_spmd.clone, body=%wide.region_3.7_spmd.clone.sunk | while | flops 813369472 | bytes 27428840 | solution.py:147
  191.9 3.2 fusion.174
  205.5 3.2 fusion.174
  219.1 3.2 fusion.174
  232.7 3.2 fusion.174
  260.2 3.7 collective-permute-done.5
  264.6 4.0 multiply_add_fusion.3
  268.6 4.8 collective-permute-start.6
  277.3 3.8 multiply_add_fusion
  281.1 4.9 collective-permute-start.15
  286.1 115.2 %while.43 = (s32[]{:T(128)}, f32[2,128,512]{2,1,0:T(8,128)}, f32[3,2,128,512]{3,2,0,1:T(8,128)}, s32[]{:T(128)}, s32[]{:T(128)}, /*index=5*/s32[]{:T(128)}, s32[]{:T(128)}) while((s32[]{:T(128)}, f32[2,128,512]{2,1,0:T(8,128)}, f32[3,2,128,512]{3,2,0,1:T(8,128)}, s32[]{:T(128)}, s32[]{:T(128)}, /*index=5*/s32[]{:T(128)}, s32[]{:T(128)}) %tuple.94), condition=%wide.region_9.10_spmd, body=%wide.region_8.9_spmd.sunk | while | flops 131078 | bytes 3670183 | solution.py:244
  288.0 92.6 %collective-permute-done.1 = f32[2,128,512]{2,1,0:T(8,128)S(1)} collective-permute-done((f32[2,128,512]{2,1,0:T(8,128)}, f32[2,128,512]{2,1,0:T(8,128)S(1)}, u32[]{:S(2)}, u32[]{:S(2)}) %collective-permute-start.1) | collective-permute-done | bytes 524320 | tf_op jit(solution)/shard_map/while/body/eval_jaxpr/ppermute | solution.py:12
  382.5 5.2 collective-permute-start.1
  387.7 11.7 %collective-permute-done.1 = f32[2,128,512]{2,1,0:T(8,128)S(1)} collective-permute-done((f32[2,128,512]{2,1,0:T(8,128)}, f32[2,128,512]{2,1,0:T(8,128)S(1)}, u32[]{:S(2)}, u32[]{:S(2)}) %collective-permute-start.1) | collective-permute-done | bytes 524320 | tf_op jit(solution)/shard_map/while/body/eval_jaxpr/ppermute | solution.py:12
  404.7 3.1 fusion.115
  410.1 3.9 multiply_add_fusion.2
  416.0 3.7 fusion.75
  419.7 4.5 collective-permute-start.14
  426.1 80.8 %collective-permute-done.7 = f32[32]{0:T(128)S(1)} collective-permute-done((f32[32]{0:T(128)S(1)}, f32[32]{0:T(128)S(1)}, u32[]{:S(2)}, u32[]{:S(2)}) %collective-permute-start.7) | collective-permute-done | bytes 160 | tf_op jit(solution)/shard_map/ppermute | solution.py:12
  513.7 3.4 fusion.72
  519.4 3.4 fusion.74
  (183 shorter events, 116.6 us)
Async XLA Ops:
  0.6 14.6 %copy-start = (bf16[128,4096]{1,0:T(8,128)(2,1)S(1)}, bf16[128,4096]{1,0:T(8,128)(2,1)}, u32[]{:S(2)}) copy-start(bf16[128,4096]{1,0:T(8,128)(2,1)} %param.18) | copy-start | bytes 3145732
  6.0 4.2 copy-start.3
  10.2 94.5 %collective-permute-start.9 = (f32[32,128,128]{2,1,0:T(8,128)}, f32[32,128,128]{2,1,0:T(8,128)}, u32[]{:S(2)}, u32[]{:S(2)}) collective-permute-start(f32[32,128,128]{2,1,0:T(8,128)} %fusion.77), channel_id=1, source_target_pairs={{4,0},{8,4},{12,8},{16,12},{20,16},{24,20},{28,24},{5,1},{9,5},{13... | collective-permute-start | bytes 6291464 | tf_op jit(solution)/shard_map/ppermute | solution.py:12
  15.2 97.4 %copy-start.19 = (bf16[128,512]{1,0:T(8,128)(2,1)S(1)}, bf16[128,512]{1,0:T(8,128)(2,1)}, u32[]{:S(2)}) copy-start(bf16[128,512]{1,0:T(8,128)(2,1)} %param.24) | copy-start | bytes 393220
  15.2 97.4 %copy-start.20 = (bf16[128,512]{1,0:T(8,128)(2,1)S(1)}, bf16[128,512]{1,0:T(8,128)(2,1)}, u32[]{:S(2)}) copy-start(bf16[128,512]{1,0:T(8,128)(2,1)} %param.23) | copy-start | bytes 393220
  17.0 163.5 %collective-permute-start.2 = (f32[32,128,128]{2,1,0:T(8,128)}, f32[32,128,128]{2,1,0:T(8,128)}, u32[]{:S(2)}, u32[]{:S(2)}) collective-permute-start(f32[32,128,128]{2,1,0:T(8,128)} %fusion.76), channel_id=1, source_target_pairs={{0,4},{4,8},{8,12},{12,16},{16,20},{20,24},{24,28},{1,5},{5,9},{9,... | collective-permute-start | bytes 6291464 | tf_op jit(solution)/shard_map/ppermute | solution.py:12
  104.7 80.0 %collective-permute-start.11 = (f32[32,128,128]{2,1,0:T(8,128)}, f32[32,128,128]{2,1,0:T(8,128)}, u32[]{:S(2)}, u32[]{:S(2)}) collective-permute-start(f32[32,128,128]{2,1,0:T(8,128)} %collective-permute-done.9), channel_id=1, source_target_pairs={{4,0},{8,4},{12,8},{16,12},{20,16},{24,20},{28,24},{5,1},{9,5},{13... | collective-permute-start | bytes 6291464 | tf_op jit(solution)/shard_map/ppermute | solution.py:12
  106.7 66.9 %collective-permute-start.10 = (f32[32]{0:T(128)}, f32[32]{0:T(128)S(1)}, u32[]{:S(2)}, u32[]{:S(2)}) collective-permute-start(f32[32]{0:T(128)} %slice_bitcast_fusion.3), channel_id=1, source_target_pairs={{4,0},{8,4},{12,8},{16,12},{20,16},{24,20},{28,24},{5,1},{9,5},{13... | collective-permute-start | bytes 392 | tf_op jit(solution)/shard_map/ppermute | solution.py:12
  110.5 147.1 %collective-permute-start.3 = (f32[32]{0:T(128)}, f32[32]{0:T(128)}, u32[]{:S(2)}, u32[]{:S(2)}) collective-permute-start(f32[32]{0:T(128)} %slice_bitcast_fusion.3), channel_id=1, source_target_pairs={{0,4},{4,8},{8,12},{12,16},{16,20},{20,24},{24,28},{1,5},{5,9},{9,... | collective-permute-start | bytes 392 | tf_op jit(solution)/shard_map/ppermute | solution.py:12
  112.6 45.2 %collective-permute-start = (bf16[2,128,512]{2,1,0:T(8,128)(2,1)S(1)}, bf16[2,128,512]{2,1,0:T(8,128)(2,1)S(1)}, u32[]{:S(2)}, u32[]{:S(2)}) collective-permute-start(bf16[2,128,512]{2,1,0:T(8,128)(2,1)S(1)} %get-tuple-element.388), channel_id=1, source_target_pairs={{0,4},{4,8},{8,12},{12,16},{16,20},{20,24},{24,28},{1,5},{5,9},{9,... | collective-permute-start | bytes 786440 | tf_op jit(solution)/shard_map/while/body/eval_jaxpr/ppermute | solution.py:12
  157.9 11.0 %collective-permute-start = (bf16[2,128,512]{2,1,0:T(8,128)(2,1)S(1)}, bf16[2,128,512]{2,1,0:T(8,128)(2,1)S(1)}, u32[]{:S(2)}, u32[]{:S(2)}) collective-permute-start(bf16[2,128,512]{2,1,0:T(8,128)(2,1)S(1)} %get-tuple-element.388), channel_id=1, source_target_pairs={{0,4},{4,8},{8,12},{12,16},{16,20},{20,24},{24,28},{1,5},{5,9},{9,... | collective-permute-start | bytes 786440 | tf_op jit(solution)/shard_map/while/body/eval_jaxpr/ppermute | solution.py:12
  173.6 5.7 %copy-start.22 = (f32[32]{0:T(128)}, f32[32]{0:T(128)S(1)}, u32[]{:S(2)}) copy-start(f32[32]{0:T(128)S(1)} %collective-permute-done.10) | copy-start | bytes 388
  173.6 5.7 %collective-permute-start.12 = (f32[32]{0:T(128)S(1)}, f32[32]{0:T(128)}, u32[]{:S(2)}, u32[]{:S(2)}) collective-permute-start(f32[32]{0:T(128)S(1)} %collective-permute-done.10), channel_id=1, source_target_pairs={{4,0},{8,4},{12,8},{16,12},{20,16},{24,20},{28,24},{5,1},{9,5},{13... | collective-permute-start | bytes 392 | tf_op jit(solution)/shard_map/ppermute | solution.py:12
  180.5 84.1 %collective-permute-start.4 = (f32[32,128,128]{2,1,0:T(8,128)}, f32[32,128,128]{2,1,0:T(8,128)}, u32[]{:S(2)}, u32[]{:S(2)}) collective-permute-start(f32[32,128,128]{2,1,0:T(8,128)} %collective-permute-done.2), channel_id=1, source_target_pairs={{0,4},{4,8},{8,12},{12,16},{16,20},{20,24},{24,28},{1,5},{5,9},{9,... | collective-permute-start | bytes 6291464 | tf_op jit(solution)/shard_map/ppermute | solution.py:12
  188.6 88.7 %collective-permute-start.13 = (f32[32,128,128]{2,1,0:T(8,128)}, f32[32,128,128]{2,1,0:T(8,128)}, u32[]{:S(2)}, u32[]{:S(2)}) collective-permute-start(f32[32,128,128]{2,1,0:T(8,128)} %multiply_add_fusion.1), channel_id=1, source_target_pairs={{8,0},{12,4},{16,8},{20,12},{24,16},{28,20},{9,1},{13,5},{17,9},{2... | collective-permute-start | bytes 6291464 | tf_op jit(solution)/shard_map/ppermute | solution.py:12
  191.0 4.1 copy-start.8
  204.5 4.1 copy-start.8
  218.1 4.1 copy-start.8
  231.8 4.1 copy-start.8
  252.8 4.7 copy-start.18
  252.8 7.4 %copy-start.17 = (f32[128,32]{1,0:T(8,128)S(1)}, f32[128,32]{1,0:T(8,128)}, u32[]{:S(2)}) copy-start(f32[128,32]{1,0:T(8,128)} %get-tuple-element.267) | copy-start | bytes 49156
  257.6 6.4 %collective-permute-start.5 = (f32[32]{0:T(128)}, f32[32]{0:T(128)S(1)}, u32[]{:S(2)}, u32[]{:S(2)}) collective-permute-start(f32[32]{0:T(128)} %collective-permute-done.3), channel_id=1, source_target_pairs={{0,4},{4,8},{8,12},{12,16},{16,20},{20,24},{24,28},{1,5},{5,9},{9,... | collective-permute-start | bytes 392 | tf_op jit(solution)/shard_map/ppermute | solution.py:12
  264.6 10.7 %copy-start.4 = (bf16[128,4096]{0,1:T(8,128)(2,1)S(1)}, bf16[128,4096]{0,1:T(8,128)(2,1)}, u32[]{:S(2)}) copy-start(bf16[128,4096]{0,1:T(8,128)(2,1)} %copy-done.3) | copy-start | bytes 3145732
  268.6 141.5 %collective-permute-start.6 = (f32[32,128,128]{2,1,0:T(8,128)}, f32[32,128,128]{2,1,0:T(8,128)}, u32[]{:S(2)}, u32[]{:S(2)}) collective-permute-start(f32[32,128,128]{2,1,0:T(8,128)} %multiply_add_fusion.3), channel_id=1, source_target_pairs={{0,8},{4,12},{8,16},{12,20},{16,24},{20,28},{1,9},{5,13},{9,17},{1... | collective-permute-start | bytes 6291464 | tf_op jit(solution)/shard_map/ppermute | solution.py:12
  281.1 225.8 %collective-permute-start.15 = (f32[32,128,128]{2,1,0:T(8,128)}, f32[32,128,128]{2,1,0:T(8,128)}, u32[]{:S(2)}, u32[]{:S(2)}) collective-permute-start(f32[32,128,128]{2,1,0:T(8,128)} %multiply_add_fusion), channel_id=1, source_target_pairs={{16,0},{20,4},{24,8},{28,12},{17,1},{21,5},{25,9},{29,13},{18,2},{... | collective-permute-start | bytes 6291464 | tf_op jit(solution)/shard_map/ppermute | solution.py:12
  286.1 94.6 %collective-permute-start.1 = (f32[2,128,512]{2,1,0:T(8,128)}, f32[2,128,512]{2,1,0:T(8,128)S(1)}, u32[]{:S(2)}, u32[]{:S(2)}) collective-permute-start(f32[2,128,512]{2,1,0:T(8,128)} %get-tuple-element.439), channel_id=1, source_target_pairs={{4,0},{8,4},{12,8},{16,12},{20,16},{24,20},{28,24},{5,1},{9,5},{13... | collective-permute-start | bytes 1572872 | tf_op jit(solution)/shard_map/while/body/eval_jaxpr/ppermute | solution.py:12
  382.5 16.8 %collective-permute-start.1 = (f32[2,128,512]{2,1,0:T(8,128)}, f32[2,128,512]{2,1,0:T(8,128)S(1)}, u32[]{:S(2)}, u32[]{:S(2)}) collective-permute-start(f32[2,128,512]{2,1,0:T(8,128)} %get-tuple-element.439), channel_id=1, source_target_pairs={{4,0},{8,4},{12,8},{16,12},{20,16},{24,20},{28,24},{5,1},{9,5},{13... | collective-permute-start | bytes 1572872 | tf_op jit(solution)/shard_map/while/body/eval_jaxpr/ppermute | solution.py:12
  410.1 6.0 %copy-start.5 = (bf16[128,4096]{0,1:T(8,128)(2,1)S(1)}, bf16[128,4096]{0,1:T(8,128)(2,1)}, u32[]{:S(2)}) copy-start(bf16[128,4096]{0,1:T(8,128)(2,1)} %copy-done.3) | copy-start | bytes 3145732
  414.0 105.3 %collective-permute-start.8 = (f32[32,128,128]{2,1,0:T(8,128)}, f32[32,128,128]{2,1,0:T(8,128)}, u32[]{:S(2)}, u32[]{:S(2)}) collective-permute-start(f32[32,128,128]{2,1,0:T(8,128)} %multiply_add_fusion.2), channel_id=1, source_target_pairs={{0,16},{4,20},{8,24},{12,28},{1,17},{5,21},{9,25},{13,29},{2,18},{... | collective-permute-start | bytes 6291464 | tf_op jit(solution)/shard_map/ppermute | solution.py:12
  416.0 3.7 copy-start.21
  419.7 6.4 %collective-permute-start.14 = (f32[32]{0:T(128)S(1)}, f32[32]{0:T(128)S(1)}, u32[]{:S(2)}, u32[]{:S(2)}) collective-permute-start(f32[32]{0:T(128)S(1)} %copy-done.21), channel_id=1, source_target_pairs={{8,0},{12,4},{16,8},{20,12},{24,16},{28,20},{9,1},{13,5},{17,9},{2... | collective-permute-start | bytes 392 | tf_op jit(solution)/shard_map/ppermute | solution.py:12
  424.2 82.7 %collective-permute-start.7 = (f32[32]{0:T(128)S(1)}, f32[32]{0:T(128)S(1)}, u32[]{:S(2)}, u32[]{:S(2)}) collective-permute-start(f32[32]{0:T(128)S(1)} %get-tuple-element.257), channel_id=1, source_target_pairs={{0,8},{4,12},{8,16},{12,20},{16,24},{20,28},{1,9},{5,13},{9,17},{1... | collective-permute-start | bytes 392 | tf_op jit(solution)/shard_map/ppermute | solution.py:12
  (21 other events, 42.3 us)
where the time goes:
time: 526 us; the launch traced here: 524 us
  waiting for transfers between devices  321 us (61%)
  matrix products  68.1 us (13%)
  starting transfers between devices  59.9 us (11%)
  local copies, waits for them, and re-layouts  39.7 us (8%)
  other arithmetic  33.9 us (6%)
    ppermute x18, waiting for transfers between devices, passed_along(): return lax.ppermute(shard, axis, pairs)  321 us
    ppermute x18, starting transfers between devices, passed_along(): return lax.ppermute(shard, axis, pairs)  59.9 us
    add x4, other arithmetic, combine_states(): later[0] + jnp.exp(later[1])[:, None, None] * earlier[0]  15.5 us
    unnamed x46, local copies, waits for them, and re-layouts  13.1 us
    sub x4, matrix products, one_group(): expo = jnp.exp(score - peak)  12.6 us
  transfers between devices with their start and end apart: 18, of which 7 were waited for; matrix products, arithmetic and copies ran while one was open for 24% of the time, Pallas kernels for 0%

commit v1 on v0

v1 whole, which is shorter than its diff:
```python
import functools

import jax
import jax.numpy as jnp
from jax import lax
from jax.experimental import pallas as pl
from jax.experimental.pallas import tpu as pltpu
from jax.sharding import PartitionSpec as P

G = 4
WINDOW = 3
CH = 2
LAG = 1
SOFT_DELAY = 2
F32 = jnp.float32
BF16 = jnp.bfloat16


def dot(a, b, ca, cb):
    return lax.dot_general(a, b, (((ca,), (cb,)), ((), ())), preferred_element_type=F32)


def kernel(
    n,
    q_ref,
    k_ref,
    v_ref,
    do_ref,
    cum_ref,
    sq_ref,
    sk_ref,
    sv_ref,
    sdo_ref,
    lq_out,
    lk_out,
    lv_out,
    sq_out,
    sk_out,
    sv_out,
    mg_s,
    ms_s,
    ks_s,
    gs_s,
    fin,
    fout,
    gin,
    gout,
    kvin,
    kcat,
    vcat,
    acc,
    gland,
    fsend,
    frecv,
    bsend,
    brecv,
    kvsend,
    kvrecv,
    gsend,
    grecv,
):
    T = q_ref.shape[0]
    D = T
    H = cum_ref.shape[0]
    NC = H // CH
    share = H // G
    per_group = share // CH
    me = lax.axis_index("ctx")
    scale = 1.0 / D
    sscale = D ** (-0.5)

    def there(offset):
        return (me + offset >= 0) & (me + offset < n)

    def device(offset):
        if offset > 0:
            return {"ctx": jnp.where(me + offset < n, me + offset, me - offset)}
        return {"ctx": jnp.where(me + offset >= 0, me + offset, me - offset)}

    def remote(src, dst, send, recv, offset):
        return pltpu.make_async_remote_copy(
            src_ref=src,
            dst_ref=dst,
            send_sem=send,
            recv_sem=recv,
            device_id=device(offset),
            device_id_type=pl.DeviceIdType.MESH,
        )

    def fwd_copy(c):
        part = pl.ds(c * CH, CH)
        return remote(fout.at[part], fin.at[part], fsend.at[c], frecv.at[c], 1)

    def bwd_copy(c):
        part = pl.ds(c * CH, CH)
        return remote(gout.at[part], gin.at[part], bsend.at[c], brecv.at[c], -1)

    def kv_copy(slot, which):
        src = sk_ref if which == 0 else sv_ref
        i = slot * 2 + which
        return remote(src, kvin.at[slot, which], kvsend.at[i], kvrecv.at[i], slot + 1)

    def grad_copy(slot, g):
        return remote(
            acc.at[slot + 1, g], gland.at[slot, g], gsend.at[slot, g], grecv.at[slot, g], -(slot + 1)
        )

    barrier = pltpu.get_barrier_semaphore()
    for offset in (-2, -1, 1, 2):

        @pl.when(there(offset))
        def _():
            pl.semaphore_signal(
                barrier, inc=1, device_id=device(offset), device_id_type=pl.DeviceIdType.MESH
            )

    peers = jnp.minimum(me, 2) + jnp.minimum(n - 1 - me, 2)
    pl.semaphore_wait(barrier, peers)

    for slot in range(2):

        @pl.when(there(slot + 1))
        def _():
            kv_copy(slot, 0).start()
            kv_copy(slot, 1).start()

        @pl.when(jnp.logical_not(there(-slot - 1)))
        def _():
            kvin[slot] = jnp.zeros(kvin.shape[1:], BF16)

        @pl.when(jnp.logical_not(there(slot + 1)))
        def _():
            gland[slot] = jnp.zeros(gland.shape[1:], F32)

    @pl.when(me == 0)
    def _():
        fin[...] = jnp.zeros(fin.shape, BF16)

    @pl.when(me == n - 1)
    def _():
        gin[...] = jnp.zeros(gin.shape, BF16)

    acc[...] = jnp.zeros(acc.shape, F32)

    rows_i = lax.broadcasted_iota(jnp.int32, (T, T), 0)
    cols_i = lax.broadcasted_iota(jnp.int32, (T, T), 1)

    def cols(h):
        return pl.ds(pl.multiple_of(h * D, D), D)

    def fades(h):
        row = cum_ref[h]
        wide = jnp.broadcast_to(row, (T, T))
        tall = wide.T
        return row[:, T - 1 : T], wide, tall

    def local(c):
        for j in range(CH):
            h = c * CH + j
            at = cols(h)
            total, wide, tall = fades(h)
            decay = jnp.where(rows_i >= cols_i, jnp.exp(jnp.minimum(tall - wide, 0.0)), 0.0)
            q, k, v, do = q_ref[:, at], k_ref[:, at], v_ref[:, at], do_ref[:, at]
            wk = (k.astype(F32) * jnp.exp(total - tall)).astype(BF16)
            wq = (q.astype(F32) * jnp.exp(tall)).astype(BF16)
            ks_s[h] = dot(wk, v, 0, 0)
            gs_s[h] = dot(wq, do, 0, 0)
            mg_s[h] = (decay * dot(do, v, 1, 1) * scale).astype(BF16)
            ms_s[h] = (decay * dot(q, k, 1, 1) * scale).astype(BF16)

    def pass_state(c, state, arrived, out):
        for j in range(CH):
            h = c * CH + j
            row = cum_ref[h]
            out[h] = (state[h] + jnp.exp(row[:, T - 1 : T]) * arrived[h].astype(F32)).astype(BF16)

    def fwd_pass(c):
        @pl.when(there(-1))
        def _():
            fwd_copy(c).wait_recv()

        @pl.when(there(1))
        def _():
            pass_state(c, ks_s, fin, fout)
            fwd_copy(c).start()

    def bwd_pass(c):
        @pl.when(there(1))
        def _():
            bwd_copy(c).wait_recv()

        @pl.when(there(-1))
        def _():
            pass_state(c, gs_s, gin, gout)
            bwd_copy(c).start()

    def fwd_finish(c):
        for j in range(CH):
            h = c * CH + j
            at = cols(h)
            total, wide, tall = fades(h)
            inner = dot(mg_s[h], k_ref[:, at], 1, 0)
            outer = dot(do_ref[:, at], fin[h], 1, 1)
            lq_out[:, at] = (inner + scale * jnp.exp(tall) * outer).astype(BF16)

    def bwd_finish(c):
        for j in range(CH):
            h = c * CH + j
            at = cols(h)
            total, wide, tall = fades(h)
            to_end = scale * jnp.exp(total - tall)
            lk_out[:, at] = (
                dot(mg_s[h], q_ref[:, at], 0, 0) + to_end * dot(v_ref[:, at], gin[h], 1, 1)
            ).astype(BF16)
            lv_out[:, at] = (
                dot(ms_s[h], do_ref[:, at], 0, 0) + to_end * dot(k_ref[:, at], gin[h], 1, 0)
            ).astype(BF16)

    def soft_begin():
        for slot in range(2):

            @pl.when(there(-slot - 1))
            def _():
                kv_copy(slot, 0).wait_recv()
                kv_copy(slot, 1).wait_recv()

        for g in range(G):
            at = slice(g * D, (g + 1) * D)
            kcat[g, 0:T] = sk_ref[:, at]
            vcat[g, 0:T] = sv_ref[:, at]
            for slot in range(2):
                kcat[g, (slot + 1) * T : (slot + 2) * T] = kvin[slot, 0, :, at]
                vcat[g, (slot + 1) * T : (slot + 2) * T] = kvin[slot, 1, :, at]

    span = WINDOW * T

    def soft(c):
        g = c // per_group
        k, v = kcat[g], vcat[g]
        q = jnp.concatenate([sq_ref[:, cols(c * CH + j)] for j in range(CH)], axis=0)
        do = jnp.concatenate([sdo_ref[:, cols(c * CH + j)] for j in range(CH)], axis=0)
        t = lax.broadcasted_iota(jnp.int32, (CH * T, span), 0) % T
        s = lax.broadcasted_iota(jnp.int32, (CH * T, span), 1)
        visible = (s <= t) | ((s >= T) & (s < (me + 1) * T))
        score = jnp.where(visible, dot(q, k, 1, 1) * sscale, -jnp.inf)
        peak = jnp.max(score, axis=1, keepdims=True)
        expo = jnp.exp(score - peak)
        prob = expo * (1.0 / jnp.sum(expo, axis=1, keepdims=True))
        half = prob.astype(BF16)
        out = dot(half, v, 1, 0).astype(BF16)
        delta = jnp.sum(do.astype(F32) * out.astype(F32), axis=1, keepdims=True)
        ds = (prob * (dot(do, v, 1, 1) - delta)).astype(BF16)
        dq = (dot(ds, k, 1, 0) * sscale).astype(BF16)
        for j in range(CH):
            sq_out[:, cols(c * CH + j)] = dq[j * T : (j + 1) * T]
        dk = dot(ds, q, 0, 0) * sscale
        dv = dot(half, do, 0, 0)
        for slot in range(WINDOW):
            acc[slot, g, 0] += dk[slot * T : (slot + 1) * T]
            acc[slot, g, 1] += dv[slot * T : (slot + 1) * T]

        @pl.when(c % per_group == per_group - 1)
        def _():
            for slot in range(2):

                @pl.when(there(-slot - 1))
                def _():
                    grad_copy(slot, g).start()

    def step(s, carry):
        cf = s - LAG * me
        cb = s - LAG * (n - 1 - me)
        cs = s - SOFT_DELAY
        on_f = (cf >= 0) & (cf < NC)
        on_b = (cb >= 0) & (cb < NC)

        @pl.when(s < NC)
        def _():
            local(s)

        @pl.when(on_f)
        def _():
            fwd_pass(cf)

        @pl.when(on_b)
        def _():
            bwd_pass(cb)

        @pl.when(on_f)
        def _():
            fwd_finish(cf)

        @pl.when(on_b)
        def _():
            bwd_finish(cb)

        @pl.when(cs == 0)
        def _():
            soft_begin()

        @pl.when((cs >= 0) & (cs < NC))
        def _():
            soft(cs)

        return carry

    lax.fori_loop(0, NC + max(LAG * (n - 1), SOFT_DELAY), step, 0)

    for g in range(G):
        at = slice(g * D, (g + 1) * D)
        for slot in range(2):

            @pl.when(there(slot + 1))
            def _():
                grad_copy(slot, g).wait_recv()

        sk_out[:, at] = (acc[0, g, 0] + gland[0, g, 0] + gland[1, g, 0]).astype(BF16)
        sv_out[:, at] = (acc[0, g, 1] + gland[0, g, 1] + gland[1, g, 1]).astype(BF16)

    def drain(c, carry):
        @pl.when(there(1))
        def _():
            fwd_copy(c).wait_send()

        @pl.when(there(-1))
        def _():
            bwd_copy(c).wait_send()

        return carry

    lax.fori_loop(0, NC, drain, 0)
    for slot in range(2):

        @pl.when(there(slot + 1))
        def _():
            kv_copy(slot, 0).wait_send()
            kv_copy(slot, 1).wait_send()

        @pl.when(there(-slot - 1))
        def _():
            for g in range(G):
                grad_copy(slot, g).wait_send()


def body(q, k, v, do, power, surplus, sq, sk, sv, sdo):
    n = lax.axis_size("ctx")
    T, HD = q.shape
    H = surplus.shape[1]
    D = HD // H
    NC = H // CH
    rate = surplus - jnp.power(2.0, -power.astype(F32))[None, :]
    cum = jnp.cumsum(rate, axis=0).T.reshape(H, 1, T)
    whole = jax.ShapeDtypeStruct((T, HD), BF16)
    narrow = jax.ShapeDtypeStruct(sk.shape, BF16)
    vm = pl.BlockSpec(memory_space=pltpu.VMEM)
    dma = pltpu.SemaphoreType.DMA
    return pl.pallas_call(
        functools.partial(kernel, n),
        out_shape=(whole, whole, whole, whole, narrow, narrow),
        in_specs=[vm] * 9,
        out_specs=[vm] * 6,
        scratch_shapes=[
            pltpu.VMEM((H, T, T), BF16),
            pltpu.VMEM((H, T, T), BF16),
            pltpu.VMEM((H, D, D), F32),
            pltpu.VMEM((H, D, D), F32),
            pltpu.VMEM((H, D, D), BF16),
            pltpu.VMEM((H, D, D), BF16),
            pltpu.VMEM((H, D, D), BF16),
            pltpu.VMEM((H, D, D), BF16),
            pltpu.VMEM((2, 2) + sk.shape, BF16),
            pltpu.VMEM((G, WINDOW * T, D), BF16),
            pltpu.VMEM((G, WINDOW * T, D), BF16),
            pltpu.VMEM((WINDOW, G, 2, T, D), F32),
            pltpu.VMEM((2, G, 2, T, D), F32),
            dma((NC,)),
            dma((NC,)),
            dma((NC,)),
            dma((NC,)),
            dma((4,)),
            dma((4,)),
            dma((2, G)),
            dma((2, G)),
        ],
        compiler_params=pltpu.CompilerParams(
            collective_id=0, has_side_effects=True, vmem_limit_bytes=48 * 1024 * 1024
        ),
        cost_estimate=pl.CostEstimate(
            flops=4_000_000_000, bytes_accessed=12_000_000, transcendentals=4_000_000
        ),
    )(q, k, v, do, cum, sq, sk, sv, sdo)


def solution(mesh):
    rows = P(("dp", "ctx"), None)
    return jax.shard_map(
        body,
        mesh=mesh,
        in_specs=(rows, rows, rows, rows, P("dp"), rows, rows, rows, rows, rows),
        out_specs=(rows,) * 6,
        check_vma=False,
    )
```

time: 526 us -> 121 us (0.23)
  the two profiles are of different devices: /device:TPU:16 before, /device:TPU:0 now
where the time goes in v1:
time: 121 us; the launch traced here: 120 us
  Pallas kernels  111 us (92%)
  local copies, waits for them, and re-layouts  7.21 us (6%)
  other arithmetic  1.62 us (1%)
    pallas_call x1, Pallas kernels, body(): pl.pallas_call(functools.partial(kernel, n), out_shape=(whole, whole, who...  111 us
    unnamed x12, local copies, waits for them, and re-layouts  7.06 us

profile of v1, /device:TPU:0, one launch (start us, length us, event | category | flops | bytes accessed | tf_op | source)
XLA Modules:
  0.0 120.3 jit_solution(10046896093246088807)
XLA Ops:
  0.6 0.7 negate_power_fusion
  1.3 0.8 broadcast_subtract_fusion
  2.1 0.0 copy-start.1
  2.1 0.0 copy-start.2
  2.1 0.1 copy.16
  2.2 0.2 reduce_window_sum.11
  2.4 0.1 copy.17
  2.4 0.6 copy-done.1
  3.0 0.1 copy-done.2
  3.1 0.0 copy-start
  3.1 1.2 %copy-done = bf16[128,4096]{1,0:T(8,128)(2,1)S(1)} copy-done((bf16[128,4096]{1,0:T(8,128)(2,1)S(1)}, bf16[128,4096]{1,0:T(8,128)(2,1)}, u32[]{:S(2)}) %copy-start) | copy-done | bytes 1048600
  4.3 110.8 %shard_map.145 = (bf16[128,4096]{1,0:T(8,128)(2,1)S(1)}, bf16[128,4096]{1,0:T(8,128)(2,1)S(1)}, bf16[128,4096]{1,0:T(8,128)(2,1)S(1)}, bf16[128,4096]{1,0:T(8,12...) custom-call(bf16[128,4096]{1,0:T(8,128)(2,1)S(1)} %copy-done, bf16[128,4096]{1,0:T(8,128)(2,1)} %k_ref.1, ...), custom_call_target="tpu_custom_call" | custom-call | flops 4000000000 | bytes 12000000 | tf_op jit(solution)/shard_map/pallas_call | solution.py:357
  115.1 1.0 copy.24
  116.0 1.0 copy.25
  117.0 1.0 copy.26
  118.0 1.0 copy.27
  118.9 0.7 copy.28
  119.6 0.7 copy.29
Async XLA Ops:
  2.1 0.9 copy-start.1
  2.1 1.0 copy-start.2
  3.1 1.2 %copy-start = (bf16[128,4096]{1,0:T(8,128)(2,1)S(1)}, bf16[128,4096]{1,0:T(8,128)(2,1)}, u32[]{:S(2)}) copy-start(bf16[128,4096]{1,0:T(8,128)(2,1)} %q_ref.1) | copy-start | bytes 3145732

commit v2 on v1

--- a/solution.py
+++ b/solution.py
@@ -10,8 +10,11 @@
 G = 4
 WINDOW = 3
 CH = 2
-LAG = 1
-SOFT_DELAY = 2
+LAG = 2
+FINISH_CH = 4
+SOFT_CH = 2
+SOFT_DELAY = 8
+SOFT_EVERY = 1
 F32 = jnp.float32
 BF16 = jnp.bfloat16
 
@@ -37,8 +40,9 @@
     sq_out,
     sk_out,
     sv_out,
-    mg_s,
-    ms_s,
+    rise_s,
+    fall_s,
+    tall_s,
     ks_s,
     gs_s,
     fin,
@@ -49,6 +53,7 @@
     kcat,
     vcat,
     acc,
+    gsent,
     gland,
     fsend,
     frecv,
@@ -64,7 +69,8 @@
     H = cum_ref.shape[0]
     NC = H // CH
     share = H // G
-    per_group = share // CH
+    per_group = share // SOFT_CH
+    NU = H // SOFT_CH
     me = lax.axis_index("ctx")
     scale = 1.0 / D
     sscale = D ** (-0.5)
@@ -102,7 +108,7 @@
 
     def grad_copy(slot, g):
         return remote(
-            acc.at[slot + 1, g], gland.at[slot, g], gsend.at[slot, g], grecv.at[slot, g], -(slot + 1)
+            gsent.at[slot, g], gland.at[slot, g], gsend.at[slot, g], grecv.at[slot, g], -(slot + 1)
         )
 
     barrier = pltpu.get_barrier_semaphore()
@@ -130,7 +136,7 @@
 
         @pl.when(jnp.logical_not(there(slot + 1)))
         def _():
-            gland[slot] = jnp.zeros(gland.shape[1:], F32)
+            gland[slot] = jnp.zeros(gland.shape[1:], BF16)
 
     @pl.when(me == 0)
     def _():
@@ -147,26 +153,22 @@
 
     def cols(h):
         return pl.ds(pl.multiple_of(h * D, D), D)
-
-    def fades(h):
-        row = cum_ref[h]
-        wide = jnp.broadcast_to(row, (T, T))
-        tall = wide.T
-        return row[:, T - 1 : T], wide, tall
 
     def local(c):
         for j in range(CH):
             h = c * CH + j
             at = cols(h)
-            total, wide, tall = fades(h)
-            decay = jnp.where(rows_i >= cols_i, jnp.exp(jnp.minimum(tall - wide, 0.0)), 0.0)
-            q, k, v, do = q_ref[:, at], k_ref[:, at], v_ref[:, at], do_ref[:, at]
-            wk = (k.astype(F32) * jnp.exp(total - tall)).astype(BF16)
-            wq = (q.astype(F32) * jnp.exp(tall)).astype(BF16)
-            ks_s[h] = dot(wk, v, 0, 0)
-            gs_s[h] = dot(wq, do, 0, 0)
-            mg_s[h] = (decay * dot(do, v, 1, 1) * scale).astype(BF16)
-            ms_s[h] = (decay * dot(q, k, 1, 1) * scale).astype(BF16)
+            row = cum_ref[h]
+            tall = jnp.broadcast_to(row, (T, T)).T
+            rise = jnp.exp(tall)
+            fall = jnp.exp(row[:, T - 1 : T] - tall)
+            tall_s[h] = tall
+            rise_s[h] = rise
+            fall_s[h] = fall
+            wk = (k_ref[:, at].astype(F32) * fall).astype(BF16)
+            wq = (q_ref[:, at].astype(F32) * rise).astype(BF16)
+            ks_s[h] = dot(wk, v_ref[:, at], 0, 0)
+            gs_s[h] = dot(wq, do_ref[:, at], 0, 0)
 
     def pass_state(c, state, arrived, out):
         for j in range(CH):
@@ -194,27 +196,31 @@
             pass_state(c, gs_s, gin, gout)
             bwd_copy(c).start()
 
-    def fwd_finish(c):
-        for j in range(CH):
-            h = c * CH + j
+    def finish(f):
+        results = []
+        for j in range(FINISH_CH):
+            h = f * FINISH_CH + j
             at = cols(h)
-            total, wide, tall = fades(h)
-            inner = dot(mg_s[h], k_ref[:, at], 1, 0)
-            outer = dot(do_ref[:, at], fin[h], 1, 1)
-            lq_out[:, at] = (inner + scale * jnp.exp(tall) * outer).astype(BF16)
-
-    def bwd_finish(c):
-        for j in range(CH):
-            h = c * CH + j
-            at = cols(h)
-            total, wide, tall = fades(h)
-            to_end = scale * jnp.exp(total - tall)
-            lk_out[:, at] = (
-                dot(mg_s[h], q_ref[:, at], 0, 0) + to_end * dot(v_ref[:, at], gin[h], 1, 1)
-            ).astype(BF16)
-            lv_out[:, at] = (
-                dot(ms_s[h], do_ref[:, at], 0, 0) + to_end * dot(k_ref[:, at], gin[h], 1, 0)
-            ).astype(BF16)
+            q, k, v, do = q_ref[:, at], k_ref[:, at], v_ref[:, at], do_ref[:, at]
+            key_in, grad_in = fin[h], gin[h]
+            fade = jnp.exp(jnp.minimum(tall_s[h] - cum_ref[h], 0.0))
+            decay = jnp.where(rows_i >= cols_i, fade, 0.0) * scale
+            mg = (decay * dot(do, v, 1, 1)).astype(BF16)
+            ms = (decay * dot(q, k, 1, 1)).astype(BF16)
+            rise = rise_s[h] * scale
+            fall = fall_s[h] * scale
+            results.append(
+                (
+                    at,
+                    (dot(mg, k, 1, 0) + rise * dot(do, key_in, 1, 1)).astype(BF16),
+                    (dot(mg, q, 0, 0) + fall * dot(v, grad_in, 1, 1)).astype(BF16),
+                    (dot(ms, do, 0, 0) + fall * dot(k, grad_in, 1, 0)).astype(BF16),
+                )
+            )
+        for at, a, b, c in results:
+            lq_out[:, at] = a
+            lk_out[:, at] = b
+            lv_out[:, at] = c
 
     def soft_begin():
         for slot in range(2):
@@ -237,10 +243,10 @@
     def soft(c):
         g = c // per_group
         k, v = kcat[g], vcat[g]
-        q = jnp.concatenate([sq_ref[:, cols(c * CH + j)] for j in range(CH)], axis=0)
-        do = jnp.concatenate([sdo_ref[:, cols(c * CH + j)] for j in range(CH)], axis=0)
-        t = lax.broadcasted_iota(jnp.int32, (CH * T, span), 0) % T
-        s = lax.broadcasted_iota(jnp.int32, (CH * T, span), 1)
+        q = jnp.concatenate([sq_ref[:, cols(c * SOFT_CH + j)] for j in range(SOFT_CH)], axis=0)
+        do = jnp.concatenate([sdo_ref[:, cols(c * SOFT_CH + j)] for j in range(SOFT_CH)], axis=0)
+        t = lax.broadcasted_iota(jnp.int32, (SOFT_CH * T, span), 0) % T
+        s = lax.broadcasted_iota(jnp.int32, (SOFT_CH * T, span), 1)
         visible = (s <= t) | ((s >= T) & (s < (me + 1) * T))
         score = jnp.where(visible, dot(q, k, 1, 1) * sscale, -jnp.inf)
         peak = jnp.max(score, axis=1, keepdims=True)
@@ -251,8 +257,8 @@
         delta = jnp.sum(do.astype(F32) * out.astype(F32), axis=1, keepdims=True)
         ds = (prob * (dot(do, v, 1, 1) - delta)).astype(BF16)
         dq = (dot(ds, k, 1, 0) * sscale).astype(BF16)
-        for j in range(CH):
-            sq_out[:, cols(c * CH + j)] = dq[j * T : (j + 1) * T]
+        for j in range(SOFT_CH):
+            sq_out[:, cols(c * SOFT_CH + j)] = dq[j * T : (j + 1) * T]
         dk = dot(ds, q, 0, 0) * sscale
         dv = dot(half, do, 0, 0)
         for slot in range(WINDOW):
@@ -265,12 +271,16 @@
 
                 @pl.when(there(-slot - 1))
                 def _():
+                    gsent[slot, g] = acc[slot + 1, g].astype(BF16)
                     grad_copy(slot, g).start()
+
+    RATIO = FINISH_CH // CH
 
     def step(s, carry):
         cf = s - LAG * me
         cb = s - LAG * (n - 1 - me)
         cs = s - SOFT_DELAY
+        unit = cs // SOFT_EVERY
         on_f = (cf >= 0) & (cf < NC)
         on_b = (cb >= 0) & (cb < NC)
 
@@ -286,25 +296,24 @@
         def _():
             bwd_pass(cb)
 
-        @pl.when(on_f)
-        def _():
-            fwd_finish(cf)
-
-        @pl.when(on_b)
-        def _():
-            bwd_finish(cb)
+        last = s - LAG * jnp.maximum(me, n - 1 - me)
+        unit_f = last // RATIO
+
+        @pl.when((last >= 0) & (last % RATIO == RATIO - 1) & (last < NC))
+        def _():
+            finish(unit_f)
 
         @pl.when(cs == 0)
         def _():
             soft_begin()
 
-        @pl.when((cs >= 0) & (cs < NC))
-        def _():
-            soft(cs)
+        @pl.when((cs >= 0) & (cs % SOFT_EVERY == 0) & (unit < NU))
+        def _():
+            soft(unit)
 
         return carry
 
-    lax.fori_loop(0, NC + max(LAG * (n - 1), SOFT_DELAY), step, 0)
+    lax.fori_loop(0, max(NC + LAG * (n - 1), SOFT_DELAY + SOFT_EVERY * (NU - 1) + 1), step, 0)
 
     for g in range(G):
         at = slice(g * D, (g + 1) * D)
@@ -314,8 +323,10 @@
             def _():
                 grad_copy(slot, g).wait_recv()
 
-        sk_out[:, at] = (acc[0, g, 0] + gland[0, g, 0] + gland[1, g, 0]).astype(BF16)
-        sv_out[:, at] = (acc[0, g, 1] + gland[0, g, 1] + gland[1, g, 1]).astype(BF16)
+        later = gland[0, g, 0].astype(F32) + gland[1, g, 0].astype(F32)
+        sk_out[:, at] = (acc[0, g, 0] + later).astype(BF16)
+        later = gland[0, g, 1].astype(F32) + gland[1, g, 1].astype(F32)
+        sv_out[:, at] = (acc[0, g, 1] + later).astype(BF16)
 
     def drain(c, carry):
         @pl.when(there(1))
@@ -360,8 +371,9 @@
         in_specs=[vm] * 9,
         out_specs=[vm] * 6,
         scratch_shapes=[
-            pltpu.VMEM((H, T, T), BF16),
-            pltpu.VMEM((H, T, T), BF16),
+            pltpu.VMEM((H, T, T), F32),
+            pltpu.VMEM((H, T, T), F32),
+            pltpu.VMEM((H, T, T), F32),
             pltpu.VMEM((H, D, D), F32),
             pltpu.VMEM((H, D, D), F32),
             pltpu.VMEM((H, D, D), BF16),
@@ -372,7 +384,8 @@
             pltpu.VMEM((G, WINDOW * T, D), BF16),
             pltpu.VMEM((G, WINDOW * T, D), BF16),
             pltpu.VMEM((WINDOW, G, 2, T, D), F32),
-            pltpu.VMEM((2, G, 2, T, D), F32),
+            pltpu.VMEM((2, G, 2, T, D), BF16),
+            pltpu.VMEM((2, G, 2, T, D), BF16),
             dma((NC,)),
             dma((NC,)),
             dma((NC,)),

time: 121 us -> 97.5 us (0.81)
  Pallas kernels: 111 us -> 87.7 us
    pallas_call x1, Pallas kernels: 111 us -> 87.7 us  [body(): pl.pallas_call(functools.partial(kernel, n), out_shape=(whole, whole, who...]
where the time goes in v2:
time: 97.5 us; the launch traced here: 97.2 us
  Pallas kernels  87.7 us (90%)
  local copies, waits for them, and re-layouts  7.21 us (7%)
  other arithmetic  1.62 us (2%)
    pallas_call x1, Pallas kernels, body(): pl.pallas_call(functools.partial(kernel, n), out_shape=(whole, whole, who...  87.7 us
    unnamed x12, local copies, waits for them, and re-layouts  7.06 us

profile of v2, /device:TPU:0, one launch (start us, length us, event | category | flops | bytes accessed | tf_op | source)
XLA Modules:
  0.0 97.2 jit_solution(14505307828012031196)
XLA Ops:
  0.6 0.7 negate_power_fusion
  1.3 0.8 broadcast_subtract_fusion
  2.1 0.0 copy-start.1
  2.1 0.0 copy-start.2
  2.1 0.1 copy.16
  2.2 0.2 reduce_window_sum.11
  2.4 0.1 copy.17
  2.4 0.6 copy-done.1
  3.0 0.1 copy-done.2
  3.1 0.0 copy-start
  3.1 1.2 %copy-done = bf16[128,4096]{1,0:T(8,128)(2,1)S(1)} copy-done((bf16[128,4096]{1,0:T(8,128)(2,1)S(1)}, bf16[128,4096]{1,0:T(8,128)(2,1)}, u32[]{:S(2)}) %copy-start) | copy-done | bytes 1048600
  4.3 87.7 %shard_map.145 = (bf16[128,4096]{1,0:T(8,128)(2,1)S(1)}, bf16[128,4096]{1,0:T(8,128)(2,1)S(1)}, bf16[128,4096]{1,0:T(8,128)(2,1)S(1)}, bf16[128,4096]{1,0:T(8,12...) custom-call(bf16[128,4096]{1,0:T(8,128)(2,1)S(1)} %copy-done, bf16[128,4096]{1,0:T(8,128)(2,1)} %k_ref.1, ...), custom_call_target="tpu_custom_call" | custom-call | flops 4000000000 | bytes 12000000 | tf_op jit(solution)/shard_map/pallas_call | solution.py:368
  92.0 1.0 %copy.24 = bf16[128,4096]{1,0:T(8,128)(2,1)} copy(bf16[128,4096]{1,0:T(8,128)(2,1)S(1)} %get-tuple-element.12) | data formatting | bytes 2097152
  93.0 1.0 copy.25
  94.0 1.0 copy.26
  94.9 1.0 copy.27
  95.9 0.7 copy.28
  96.6 0.7 copy.29
Async XLA Ops:
  2.1 0.9 copy-start.1
  2.1 1.0 copy-start.2
  3.1 1.2 %copy-start = (bf16[128,4096]{1,0:T(8,128)(2,1)S(1)}, bf16[128,4096]{1,0:T(8,128)(2,1)}, u32[]{:S(2)}) copy-start(bf16[128,4096]{1,0:T(8,128)(2,1)} %q_ref.1) | copy-start | bytes 3145732

commit v3 on v2

--- a/solution.py
+++ b/solution.py
@@ -9,12 +9,12 @@
 
 G = 4
 WINDOW = 3
-CH = 2
-LAG = 2
+CH = 1
+LAG = 4
 FINISH_CH = 4
 SOFT_CH = 2
-SOFT_DELAY = 8
-SOFT_EVERY = 1
+SOFT_DELAY = 20
+SOFT_EVERY = 2
 F32 = jnp.float32
 BF16 = jnp.bfloat16
 

time: 97.5 us -> 96.8 us (level)
  no operation moved by 1% of the time
where the time goes in v3:
time: 96.8 us; the launch traced here: 96.6 us
  Pallas kernels  87.1 us (90%)
  local copies, waits for them, and re-layouts  7.21 us (7%)
  other arithmetic  1.62 us (2%)
    pallas_call x1, Pallas kernels, body(): pl.pallas_call(functools.partial(kernel, n), out_shape=(whole, whole, who...  87.1 us
    unnamed x12, local copies, waits for them, and re-layouts  7.06 us

profile of v3, /device:TPU:0, one launch (start us, length us, event | category | flops | bytes accessed | tf_op | source)
XLA Modules:
  0.0 96.6 jit_solution(2666629399007768529)
XLA Ops:
  0.6 0.7 negate_power_fusion
  1.3 0.8 broadcast_subtract_fusion
  2.1 0.0 copy-start.1
  2.1 0.0 copy-start.2
  2.1 0.1 copy.16
  2.2 0.2 reduce_window_sum.11
  2.4 0.1 copy.17
  2.4 0.6 copy-done.1
  3.0 0.1 copy-done.2
  3.1 0.0 copy-start
  3.1 1.2 %copy-done = bf16[128,4096]{1,0:T(8,128)(2,1)S(1)} copy-done((bf16[128,4096]{1,0:T(8,128)(2,1)S(1)}, bf16[128,4096]{1,0:T(8,128)(2,1)}, u32[]{:S(2)}) %copy-start) | copy-done | bytes 1048600
  4.3 87.1 %shard_map.145 = (bf16[128,4096]{1,0:T(8,128)(2,1)S(1)}, bf16[128,4096]{1,0:T(8,128)(2,1)S(1)}, bf16[128,4096]{1,0:T(8,128)(2,1)S(1)}, bf16[128,4096]{1,0:T(8,12...) custom-call(bf16[128,4096]{1,0:T(8,128)(2,1)S(1)} %copy-done, bf16[128,4096]{1,0:T(8,128)(2,1)} %k_ref.1, ...), custom_call_target="tpu_custom_call" | custom-call | flops 4000000000 | bytes 12000000 | tf_op jit(solution)/shard_map/pallas_call | solution.py:368
  91.4 1.0 %copy.24 = bf16[128,4096]{1,0:T(8,128)(2,1)} copy(bf16[128,4096]{1,0:T(8,128)(2,1)S(1)} %get-tuple-element.12) | data formatting | bytes 2097152
  92.3 1.0 %copy.25 = bf16[128,4096]{1,0:T(8,128)(2,1)} copy(bf16[128,4096]{1,0:T(8,128)(2,1)S(1)} %get-tuple-element.13) | data formatting | bytes 2097152
  93.3 1.0 %copy.26 = bf16[128,4096]{1,0:T(8,128)(2,1)} copy(bf16[128,4096]{1,0:T(8,128)(2,1)S(1)} %get-tuple-element.14) | data formatting | bytes 2097152
  94.3 1.0 %copy.27 = bf16[128,4096]{1,0:T(8,128)(2,1)} copy(bf16[128,4096]{1,0:T(8,128)(2,1)S(1)} %get-tuple-element.15) | data formatting | bytes 2097152
  95.2 0.7 copy.28
  95.9 0.7 copy.29
Async XLA Ops:
  2.1 0.9 copy-start.1
  2.1 1.0 %copy-start.2 = (bf16[128,512]{1,0:T(8,128)(2,1)S(1)}, bf16[128,512]{1,0:T(8,128)(2,1)}, u32[]{:S(2)}) copy-start(bf16[128,512]{1,0:T(8,128)(2,1)} %sv_ref.1) | copy-start | bytes 393220
  3.1 1.2 %copy-start = (bf16[128,4096]{1,0:T(8,128)(2,1)S(1)}, bf16[128,4096]{1,0:T(8,128)(2,1)}, u32[]{:S(2)}) copy-start(bf16[128,4096]{1,0:T(8,128)(2,1)} %q_ref.1) | copy-start | bytes 3145732
